TPU v7x, 32 devices: a whole 2x2x4 slice. The times are simulated.
32 devices in a mesh: shot: 4 (over y, core), slab: 8 (over z, x).
Axes of the slice: x: 2, y: 2, z: 4, core: 2. Of those that a mesh axis runs over, the one named last changes fastest.
Arguments:
- source_field: bfloat16 [12, 8, 32, 256, 128], P('shot', None, 'slab'), may hold values from -4 to 4
- receiver_field: bfloat16 [12, 8, 32, 256, 128], P('shot', None, 'slab'), may hold values from -4 to 4
- shot_group: int32 [12], replicated, may hold values from 0 to 11
- first_weight: bfloat16 [32, 12, 3, 3, 3], replicated, may hold values from -0.3125 to 0.3125
- first_bias: float32 [32], replicated, may hold values from -3 to 3
- second_weight: bfloat16 [32, 32, 3, 3, 3], replicated, may hold values from -0.21875 to 0.21875
- second_bias: float32 [32], replicated, may hold values from -3 to 3
Outputs:
- features: bfloat16 [32, 32, 256, 128], P(None, 'shot', 'slab')
All inputs are finite; a program needn't handle non-finite values.
Results may differ from a plain program's by a relative error of at most 0.01.
Values may be sent and summed in bfloat16 or wider, within the bound.
A program may use at most 128 MiB of HBM per device.

v0:
```python
import jax
import jax.numpy as jnp
from jax import lax
from jax.sharding import PartitionSpec as P


def extended(block, sides, width):
    for axis, dim in sides:
        count = lax.axis_size(axis)
        forward = [(i, i + 1) for i in range(count - 1)]
        backward = [(target, source) for source, target in forward]
        low = lax.ppermute(
            lax.slice_in_dim(block, block.shape[dim] - width, None, axis=dim), axis, forward
        )
        high = lax.ppermute(lax.slice_in_dim(block, 0, width, axis=dim), axis, backward)
        block = jnp.concatenate([low, block, high], axis=dim)
    return block


def convolve(padded, weight, biases):
    result = lax.conv_general_dilated(
        padded[None],
        weight,
        (1, 1, 1),
        ((0, 0), (0, 0), (1, 1)),
        dimension_numbers=("NCDHW", "OIDHW", "NCDHW"),
        preferred_element_type=jnp.float32,
    )[0]
    return jnp.maximum(result + biases[:, None, None, None], 0.0)


def shards(
    source_field, receiver_field, shot_group, first_weight, first_bias, second_weight, second_bias
):
    shots_here = source_field.shape[0]
    groups = first_weight.shape[1]
    slab_count = lax.axis_size("slab")
    my_groups = lax.dynamic_slice_in_dim(
        shot_group, lax.axis_index("shot") * shots_here, shots_here
    )
    labels = jnp.arange(groups, dtype=jnp.int32)
    partial_image = jnp.zeros((groups,) + source_field.shape[2:], jnp.float32)
    for shot_index in range(shots_here):
        cross_term = jnp.sum(
            source_field[shot_index].astype(jnp.float32)
            * receiver_field[shot_index].astype(jnp.float32),
            axis=0,
        )
        member = (labels == my_groups[shot_index]).astype(jnp.float32)
        partial_image = partial_image + member[:, None, None, None] * cross_term[None]
    regrouped = lax.all_to_all(
        partial_image.astype(jnp.bfloat16), "slab", split_axis=2, concat_axis=1, tiled=True
    ).astype(partial_image.dtype)
    image_tile = lax.psum_scatter(
        regrouped.astype(jnp.bfloat16), "shot", scatter_dimension=1, tiled=True
    )
    padded = extended(image_tile, (("shot", 1), ("slab", 2)), 2)
    wide_hidden = convolve(padded, first_weight, first_bias)
    tile_z = image_tile.shape[1]
    tile_x = image_tile.shape[2]
    z_place = lax.axis_index("shot") * tile_z - 1 + jnp.arange(tile_z + 2, dtype=jnp.int32)
    x_place = lax.axis_index("slab") * tile_x - 1 + jnp.arange(tile_x + 2, dtype=jnp.int32)
    z_valid = (z_place >= 0) & (z_place < tile_z * lax.axis_size("shot"))
    x_valid = (x_place >= 0) & (x_place < tile_x * slab_count)
    inside = z_valid[:, None] & x_valid[None, :]
    hidden_padded = jnp.where(inside[None, :, :, None], wide_hidden, 0.0).astype(jnp.bfloat16)
    return convolve(hidden_padded, second_weight, second_bias).astype(jnp.bfloat16)


def solution(mesh):
    placed = (
        P("shot", None, "slab", None, None),
        P("shot", None, "slab", None, None),
        P(),
        P(),
        P(),
        P(),
        P(),
    )
    return jax.shard_map(
        shards, mesh=mesh, in_specs=placed, out_specs=P(None, "shot", "slab", None), check_vma=False
    )
```

profile of v0, /device:TPU:11, one launch (start us, length us, event | category | flops | bytes accessed | tf_op | source)
XLA Modules:
  0.0 305.0 jit_solution(8645236176250601244)
XLA Ops:
  6.5 0.0 copy-start
  6.5 0.0 reduce-scatter.5.cloned.1.call-start
  6.5 0.8 dynamic_slice.3
  7.3 0.7 fusion.40
  8.0 0.6 compare_convert_fusion.2
  8.6 5.8 %multiply_reduce_fusion.2 = (f32[4,256,128]{2,1,0:T(8,128)S(1)}, f32[4,256,128]{2,1,0:T(8,128)S(1)}, f32[4,256,128]{2,1,0:T(8,128)S(1)}) fusion(bf16[3,8,4,256,128]{4,3,2,1,0:T(8,128)(2,1)} %param.8, bf16[3,8,4,256,128]{4,3,2,1,0:T(8,128)(2,1)} %param.7), kind=kLoop, calls=%fused_computation.32 | loop fusion | flops 12189696 | bytes 14155776 | tf_op jit(solution)/shard_map/reduce_sum | solution.py:44
  14.4 0.3 copy.54
  14.8 0.3 copy.56
  15.1 0.3 copy.55
  15.5 1.2 compare_convert_fusion
  16.7 2.5 add_convert_fusion
  19.2 73.1 %all_to_all.18 = bf16[12,4,256,128]{3,1,0,2:T(4,128)(2,1)S(1)} all-to-all(bf16[12,4,256,128]{3,1,0,2:T(4,128)(2,1)S(1)} %add_convert_fusion), channel_id=1, replica_groups=mesh['shot'=4,'slab'=8] {'slab'}, dimensions={2} | all-to-all | bytes 6291456 | tf_op jit(solution)/shard_map/all_to_all | solution.py:51
  92.4 0.8 copy.57
  93.2 0.9 copy.58
  94.1 0.9 copy.65
  95.1 3.7 %copy.79 = bf16[4,8,384,128]{3,1,2,0:T(8,128)(2,1)} copy(bf16[4,8,384,128]{3,2,1,0:T(8,128)(2,1)S(1)} %bitcast.53) | data formatting | bytes 6291456
  98.7 0.0 reduce-scatter.5.cloned.1.call-update
  98.8 40.2 %reduce-scatter.5.cloned.1.call-done = bf16[8,49152]{1,0:T(8,128)(2,1)} async-done(((bf16[32,49152]{1,0:T(8,128)(2,1)}), bf16[8,49152]{1,0:T(8,128)(2,1)}) %reduce-scatter.5.cloned.1.call-update) | async-done | bytes 786448
  139.0 1.8 fusion.39
  140.8 2.7 collective-permute-start
  143.6 1.9 collective-permute-start.1
  145.5 1.2 copy.71
  146.8 0.0 collective-permute-done
  146.8 0.1 constant_dynamic-update-slice_fusion.1
  147.0 3.6 %collective-permute-done.1 = bf16[12,2,32,128]{3,2,1,0:T(8,128)(2,1)S(1)} collective-permute-done((bf16[12,2,32,128]{3,2,1,0:T(8,128)(2,1)S(1)}, bf16[12,2,32,128]{3,2,1,0:T(8,128)(2,1)S(1)}, u32[]{:S(2)}, u32[]{:S(2)}) %collective-permute-start.1) | collective-permute-done | bytes 196640 | tf_op jit(solution)/shard_map/ppermute | solution.py:15
  150.6 0.1 fusion.38
  150.8 3.1 %collective-permute-start.2 = (bf16[12,12,2,128]{3,2,1,0:T(2,128)(2,1)S(1)}, bf16[12,12,2,128]{3,2,1,0:T(2,128)(2,1)S(1)}, u32[]{:S(2)}, u32[]{:S(2)}) collective-permute-start(bf16[12,12,2,128]{3,2,1,0:T(2,128)(2,1)S(1)} %get-tuple-element.10), channel_id=1, source_target_pairs={{0,1},{1,2},{2,3},{3,4},{4,5},{5,6},{6,7},{8,9},{9,10},{10,11},{11... | collective-permute-start | bytes 221192 | tf_op jit(solution)/shard_map/ppermute | solution.py:12
  153.9 2.3 collective-permute-start.3
  156.2 0.1 broadcast_and_fusion
  156.3 0.0 collective-permute-done.2
  156.3 3.6 %collective-permute-done.3 = bf16[12,12,2,128]{3,2,1,0:T(2,128)(2,1)S(1)} collective-permute-done((bf16[12,12,2,128]{3,2,1,0:T(2,128)(2,1)S(1)}, bf16[12,12,2,128]{3,2,1,0:T(2,128)(2,1)S(1)}, u32[]{:S(2)}, u32[]{:S(2)}) %collective-permute-start.3) | collective-permute-done | bytes 73760 | tf_op jit(solution)/shard_map/ppermute | solution.py:15
  159.9 0.8 maximum_bitcast_fusion
  160.7 1.1 pad
  161.7 10.3 %reshape.91 = bf16[12,12,36,1,8,17]{5,4,2,1,0,3:T(8,128)(2,1)} reshape(bf16[12,12,36,1,136]{4,2,1,0,3:T(8,128)(2,1)S(1)} %pad) | data formatting | bytes 2820096 | tf_op jit(solution)/shard_map/conv_general_dilated | solution.py:21
  172.0 26.3 %copy.61 = bf16[12,12,36,1,8,17]{0,4,5,2,1,3:T(8,128)(2,1)} copy(bf16[12,12,36,1,8,17]{5,4,2,1,0,3:T(8,128)(2,1)} %reshape.91) | data formatting | bytes 2820096 | tf_op jit(solution)/shard_map/conv_general_dilated | solution.py:21
  198.3 2.0 slice.60
  200.3 0.0 copy-done.3
  200.3 0.0 copy-done.4
  200.3 0.0 copy-done.5
  200.3 36.7 %fusion.22 = bf16[10,34,1,8,17,32]{5,3,4,1,0,2:T(8,128)(2,1)} fusion(f32[32]{0:T(128)S(1)} %copy-done.4, pred[8,17]{0,1:T(8,128)(4,1)S(1)} %copy-done.5, pred[10,34]{1,0:T(8,128)(4,1)S(1)} %broadcast_and_fusion, bf16[12,12,36,1,7,2]{0,4,5,2,1,3:T(8,128)(2,1)S(1)} %slice.60, bf16[12,12,36,1,8,17]{0,4,5,2,1,3:T(8,128)(2,1)} %copy.61, ...), kind=kOutput, calls=%fused_computation.23 | convolution fusion | flops 972438528 | bytes 4535900 | tf_op jit(solution)/shard_map/conv_general_dilated | solution.py:21
  237.0 1.5 fusion.37
  238.5 0.0 copy-done
  238.5 31.0 %fusion.12 = f32[8,32,8,17,32]{4,2,3,1,0:T(8,128)S(1)} fusion(bf16[32,32,3,3,3]{1,0,4,3,2:T(8,128)(2,1)S(1)} %copy-done, bf16[10,34,1,7,1,32]{5,3,4,1,0,2:T(8,128)(2,1)S(1)} %get-tuple-element.9, bf16[10,34,1,7,1,32]{5,3,4,1,0,2:T(8,128)(2,1)S(1)} %get-tuple-element.8, bf16[10,34,1,8,17,32]{5,3,4,1,0,2:T(8,128)(2,1)} %fusion.22), kind=kOutput, calls=%fused_computation.15 | convolution fusion | flops 1941723136 | bytes 7775744 | tf_op jit(solution)/shard_map/conv_general_dilated | solution.py:21
  269.5 4.1 %copy.63 = f32[8,32,8,17,32]{4,1,3,2,0:T(8,128)S(1)} copy(f32[8,32,8,17,32]{4,2,3,1,0:T(8,128)S(1)} %fusion.12) | data formatting | bytes 8912896 | tf_op jit(solution)/shard_map/conv_general_dilated | solution.py:21
  273.6 6.2 %slice.63 = f32[8,32,1,128,32]{4,1,3,0,2:T(8,128)} slice(f32[8,32,1,136,32]{4,1,3,0,2:T(8,128)S(1)} %bitcast.49), slice={[0:8], [0:32], [0:1], [0:128], [0:32]} | slice | bytes 8388608 | tf_op jit(solution)/shard_map/conv_general_dilated | solution.py:21
  279.8 14.2 %copy.69 = f32[8,32,1,128,32]{3,1,0,4,2:T(8,128)} copy(f32[8,32,1,128,32]{4,1,3,0,2:T(8,128)} %slice.63) | data formatting | bytes 8388608
  294.0 0.0 copy-done.2
  294.0 4.1 %fusion.28 = bf16[32,8,32,128]{3,2,1,0:T(8,128)(2,1)} fusion(f32[8,32,1,128,32]{3,1,0,4,2:T(8,128)} %copy.69, f32[32]{0:T(128)S(1)} %copy-done.2), kind=kLoop, calls=%fused_computation.29 | loop fusion | flops 3145728 | bytes 6291584 | tf_op jit(solution)/shard_map/convert_element_type | solution.py:67
  (12 shorter events, 0.1 us)
Async XLA Ops:
  6.5 232.0 %copy-start = (bf16[32,32,3,3,3]{1,0,4,3,2:T(8,128)(2,1)S(1)}, bf16[32,32,3,3,3]{1,0,4,3,2:T(8,128)(2,1)}, u32[]{:S(2)}) copy-start(bf16[32,32,3,3,3]{1,0,4,3,2:T(8,128)(2,1)} %param.12) | copy-start | bytes 165892
  6.5 132.5 %reduce-scatter.5.cloned.1.call-start = ((), (), s32[]{:S(2)}) async-start(), calls=%async_computation.2 | async-start | bytes 3932160
  140.8 6.0 %collective-permute-start = (bf16[12,2,32,128]{3,2,1,0:T(8,128)(2,1)S(1)}, bf16[12,2,32,128]{3,2,1,0:T(8,128)(2,1)S(1)}, u32[]{:S(2)}, u32[]{:S(2)}) collective-permute-start(bf16[12,2,32,128]{3,2,1,0:T(8,128)(2,1)S(1)} %copy.77), channel_id=1, source_target_pairs={{0,8},{8,16},{16,24},{1,9},{9,17},{17,25},{2,10},{10,18},{18,26},{... | collective-permute-start | bytes 589832 | tf_op jit(solution)/shard_map/ppermute | solution.py:12
  143.6 7.0 %collective-permute-start.1 = (bf16[12,2,32,128]{3,2,1,0:T(8,128)(2,1)S(1)}, bf16[12,2,32,128]{3,2,1,0:T(8,128)(2,1)S(1)}, u32[]{:S(2)}, u32[]{:S(2)}) collective-permute-start(bf16[12,2,32,128]{3,2,1,0:T(8,128)(2,1)S(1)} %copy.78), channel_id=1, source_target_pairs={{8,0},{16,8},{24,16},{9,1},{17,9},{25,17},{10,2},{18,10},{26,18},{... | collective-permute-start | bytes 589832 | tf_op jit(solution)/shard_map/ppermute | solution.py:15
  150.8 5.6 %collective-permute-start.2 = (bf16[12,12,2,128]{3,2,1,0:T(2,128)(2,1)S(1)}, bf16[12,12,2,128]{3,2,1,0:T(2,128)(2,1)S(1)}, u32[]{:S(2)}, u32[]{:S(2)}) collective-permute-start(bf16[12,12,2,128]{3,2,1,0:T(2,128)(2,1)S(1)} %get-tuple-element.10), channel_id=1, source_target_pairs={{0,1},{1,2},{2,3},{3,4},{4,5},{5,6},{6,7},{8,9},{9,10},{10,11},{11... | collective-permute-start | bytes 221192 | tf_op jit(solution)/shard_map/ppermute | solution.py:12
  153.9 6.0 %collective-permute-start.3 = (bf16[12,12,2,128]{3,2,1,0:T(2,128)(2,1)S(1)}, bf16[12,12,2,128]{3,2,1,0:T(2,128)(2,1)S(1)}, u32[]{:S(2)}, u32[]{:S(2)}) collective-permute-start(bf16[12,12,2,128]{3,2,1,0:T(2,128)(2,1)S(1)} %get-tuple-element.11), channel_id=1, source_target_pairs={{1,0},{2,1},{3,2},{4,3},{5,4},{6,5},{7,6},{9,8},{10,9},{11,10},{12... | collective-permute-start | bytes 221192 | tf_op jit(solution)/shard_map/ppermute | solution.py:15
  172.0 28.3 %copy-start.3 = (bf16[32,12,3,3,3]{0,4,3,2,1:T(4,128)(2,1)S(1)}, bf16[32,12,3,3,3]{0,4,3,2,1:T(4,128)(2,1)}, u32[]{:S(2)}) copy-start(bf16[32,12,3,3,3]{0,4,3,2,1:T(4,128)(2,1)} %param.10) | copy-start | bytes 62212
  172.0 28.3 %copy-start.4 = (f32[32]{0:T(128)S(1)}, f32[32]{0:T(128)}, u32[]{:S(2)}) copy-start(f32[32]{0:T(128)} %param.11) | copy-start | bytes 388
  172.0 28.3 %copy-start.5 = (pred[8,17]{0,1:T(8,128)(4,1)S(1)}, pred[8,17]{0,1:T(8,128)(4,1)}, u32[]{:S(2)}) copy-start(pred[8,17]{0,1:T(8,128)(4,1)} %constant.40) | copy-start | bytes 412
  279.8 14.2 %copy-start.2 = (f32[32]{0:T(128)S(1)}, f32[32]{0:T(128)}, u32[]{:S(2)}) copy-start(f32[32]{0:T(128)} %param.13) | copy-start | bytes 388
  279.8 18.4 %copy-start.1 = (bf16[32,32,3,3,3]{1,0,4,3,2:T(8,128)(2,1)S(1)}, bf16[32,32,3,3,3]{1,0,4,3,2:T(8,128)(2,1)}, u32[]{:S(2)}) copy-start(bf16[32,32,3,3,3]{1,0,4,3,2:T(8,128)(2,1)} %param.12) | copy-start | bytes 165892
Sparse Core Ops, SparseCore 0:
  98.9 40.0 reduce-scatter.4
where the time goes:
time: 306 us; the launch traced here: 305 us
  local copies, waits for them, and re-layouts  77.8 us (25%)
  blocking collectives  73.1 us (24%)
  matrix products  67.6 us (22%)
  waiting for transfers between devices  47.4 us (15%)
  other arithmetic  15.2 us (5%)
  between operations  13.7 us (4%)
  starting transfers between devices  10.1 us (3%)
    all_to_all x1, blocking collectives, shards(): lax.all_to_all(partial_image.astype(jnp.bfloat16), 'slab', split_axis=2,...  73.1 us
    conv_general_dilated x2, matrix products, convolve(): lax.conv_general_dilated(padded[None], weight, (1, 1, 1), ((0, 0), (0, 0)...  67.6 us
    conv_general_dilated x5, local copies, waits for them, and re-layouts, convolve(): lax.conv_general_dilated(padded[None], weight, (1, 1, 1), ((0, 0), (0, 0)...  48.8 us
    unnamed x2, waiting for transfers between devices  40.2 us
    unnamed x20, local copies, waits for them, and re-layouts  20.3 us
    ppermute x2, waiting for transfers between devices, extended(): lax.ppermute(lax.slice_in_dim(block, 0, width, axis=dim), axis, backward)  7.21 us
  transfers between devices with their start and end apart: 5, of which 3 were waited for; matrix products, arithmetic and copies ran while one was open for 0% of the time, Pallas kernels for 0%

commit v1 on v0

v1 whole, which is shorter than its diff:
```python
import functools

import jax
import jax.numpy as jnp
from jax import lax
from jax.experimental import pallas as pl
from jax.experimental.pallas import tpu as pltpu
from jax.sharding import PartitionSpec as P

WIDE = 6
OUT = 8


def extended(block, sides, width):
    for axis, dim in sides:
        count = lax.axis_size(axis)
        forward = [(i, i + 1) for i in range(count - 1)]
        backward = [(target, source) for source, target in forward]
        low = lax.ppermute(
            lax.slice_in_dim(block, block.shape[dim] - width, None, axis=dim), axis, forward
        )
        high = lax.ppermute(lax.slice_in_dim(block, 0, width, axis=dim), axis, backward)
        block = jnp.concatenate([low, block, high], axis=dim)
    return block


def banded(weight, count):
    rows = [
        jnp.pad(weight, ((0, 0), (0, 0), (i, count - 1 - i), (0, 0))) for i in range(count)
    ]
    return jnp.stack(rows), rows[0].shape[1] * rows[0].shape[2] * rows[0].shape[3]


def conv_kernel(tile_z, tile_x, shot_count, slab_count, place, img, w1, b1, w2, b2, out, wide, hidden):
    half = tile_z // 2
    y = img.shape[3]
    lanes = 2 * y
    lane = lax.broadcasted_iota(jnp.int32, (1, lanes), 1)
    upper = (lane >= y).astype(jnp.int32)
    cell = lane - upper * y
    first = cell == 0
    last = cell == y - 1
    channels = w1.shape[0] // WIDE

    def three(values):
        left = jnp.where(first, 0.0, pltpu.roll(values, 1, 1))
        right = jnp.where(last, 0.0, pltpu.roll(values, lanes - 1, 1))
        return [v.astype(jnp.bfloat16) for v in (left, values, right)]

    depth = img.shape[2]

    @pl.loop(0, half + 4)
    def _(z):
        for x in range(img.shape[1]):
            pair = jnp.concatenate(
                [img[z, x].astype(jnp.float32), img[z + half, x].astype(jnp.float32)], axis=1
            )
            for k, part in enumerate(three(pair)):
                wide[z, x, k * depth:(k + 1) * depth, :] = part

    z_base = place[0] * tile_z - 1
    x_base = place[1] * tile_x - 1
    hidden_x = hidden.shape[1]

    @pl.loop(0, half + 2)
    def _(z):
        z_place = z_base + z + upper * half
        z_valid = jnp.logical_and(z_place >= 0, z_place < tile_z * shot_count)
        for g in range(hidden_x // WIDE):
            window = wide[pl.ds(z, 3), g * WIDE:g * WIDE + WIDE + 2]
            got = jnp.dot(
                w1[...], window.reshape(-1, lanes), preferred_element_type=jnp.float32
            )
            for i in range(WIDE):
                x = g * WIDE + i
                x_place = x_base + x
                x_valid = jnp.logical_and(x_place >= 0, x_place < tile_x * slab_count)
                valid = jnp.logical_and(z_valid, x_valid)
                value = jnp.maximum(got[i * channels:(i + 1) * channels] + b1[...], 0.0)
                value = jnp.where(valid, value, 0.0)
                for k, part in enumerate(three(value)):
                    hidden[z, x, k * channels:(k + 1) * channels, :] = part

    out_channels = out.shape[0]
    chunk = min(16, tile_x)

    @pl.loop(0, half)
    def _(z):
        for c in range(tile_x // chunk):
            parts = []
            for g in range(chunk // OUT):
                x = c * chunk + g * OUT
                window = hidden[pl.ds(z, 3), x:x + OUT + 2]
                got = jnp.dot(
                    w2[...], window.reshape(-1, lanes), preferred_element_type=jnp.float32
                )
                parts.append(jnp.maximum(got + b2[...], 0.0))
            for h in range(2):
                pieces = [
                    p[:, h * y:(h + 1) * y].reshape(out_channels, OUT, y) for p in parts
                ]
                block = pieces[0] if len(pieces) == 1 else jnp.concatenate(pieces, axis=1)
                out[:, z + h * half, c * chunk:(c + 1) * chunk, :] = block.astype(out.dtype)


def convolutions(image, first_weight, first_bias, second_weight, second_bias, tile_z, tile_x):
    shot_count, slab_count = lax.axis_size("shot"), lax.axis_size("slab")
    channels, inputs = first_weight.shape[:2]
    out_channels = second_weight.shape[0]
    y = image.shape[3]
    depth = image.shape[2]
    half = tile_z // 2
    hidden_x = -(-(tile_x + 2) // WIDE) * WIDE
    w1 = jnp.transpose(first_weight, (0, 2, 3, 4, 1))
    w1 = jnp.pad(w1, ((0, 0),) * 4 + ((0, depth - inputs),)).reshape(channels, 3, 3, 3 * depth)
    w1, k1 = banded(w1, WIDE)
    w1 = w1.reshape(WIDE * channels, k1)
    w2 = jnp.transpose(second_weight, (0, 2, 3, 4, 1)).reshape(out_channels, 3, 3, 3 * channels)
    w2, k2 = banded(w2, OUT)
    w2 = jnp.transpose(w2, (1, 0, 2, 3, 4)).reshape(out_channels * OUT, k2)
    b1 = first_bias[:, None]
    b2 = jnp.repeat(second_bias, OUT)[:, None]
    place = jnp.stack([lax.axis_index("shot"), lax.axis_index("slab")]).astype(jnp.int32)
    vmem = pl.BlockSpec(memory_space=pltpu.VMEM)
    return pl.pallas_call(
        functools.partial(conv_kernel, tile_z, tile_x, shot_count, slab_count),
        out_shape=jax.ShapeDtypeStruct((out_channels, tile_z, tile_x, y), jnp.bfloat16),
        in_specs=[pl.BlockSpec(memory_space=pltpu.SMEM)] + [vmem] * 5,
        out_specs=vmem,
        scratch_shapes=[
            pltpu.VMEM((half + 4, image.shape[1], 3 * depth, 2 * y), jnp.bfloat16),
            pltpu.VMEM((half + 2, hidden_x, 3 * channels, 2 * y), jnp.bfloat16),
        ],
        compiler_params=pltpu.CompilerParams(vmem_limit_bytes=48 * 1024 * 1024),
        name="convolutions",
    )(place, image, w1, b1, w2, b2)


def shards(
    source_field, receiver_field, shot_group, first_weight, first_bias, second_weight, second_bias
):
    shots_here, _, slab_z, all_x, _ = source_field.shape
    shot_count, slab_count = lax.axis_size("shot"), lax.axis_size("slab")
    tile_z = slab_z * slab_count // shot_count
    tile_x = all_x // slab_count
    cross = jnp.sum(
        source_field.astype(jnp.float32) * receiver_field.astype(jnp.float32), axis=1
    ).astype(jnp.bfloat16)
    rows = lax.all_to_all(cross, "slab", split_axis=2, concat_axis=1, tiled=True)
    tile = lax.all_to_all(rows, "shot", split_axis=1, concat_axis=0, tiled=True)
    padded = extended(tile, (("shot", 1), ("slab", 2)), 2)
    hidden_x = -(-(tile_x + 2) // WIDE) * WIDE
    image = jnp.transpose(padded, (1, 2, 0, 3))
    shots = image.shape[2]
    depth = -(-shots // 16) * 16
    image = jnp.pad(
        image, ((0, 0), (0, hidden_x + 2 - image.shape[1]), (0, depth - shots), (0, 0))
    )
    weight_of_shot = jnp.take(first_weight, shot_group, axis=1)
    return convolutions(
        image, weight_of_shot, first_bias, second_weight, second_bias, tile_z, tile_x
    )


def solution(mesh):
    placed = (
        P("shot", None, "slab", None, None),
        P("shot", None, "slab", None, None),
        P(),
        P(),
        P(),
        P(),
        P(),
    )
    return jax.shard_map(
        shards, mesh=mesh, in_specs=placed, out_specs=P(None, "shot", "slab", None), check_vma=False
    )
```

time: 306 us -> 99.9 us (0.33)
  the two profiles are of different devices: /device:TPU:11 before, /device:TPU:1 now
where the time goes in v1:
time: 99.9 us; the launch traced here: 99.4 us
  local copies, waits for them, and re-layouts  28.2 us (28%)
  waiting for transfers between devices  24.1 us (24%)
  starting transfers between devices  21.8 us (22%)
  Pallas kernels  17.4 us (17%)
  other arithmetic  7.41 us (7%)
    pallas_call x1, Pallas kernels, convolutions(): pl.pallas_call(functools.partial(conv_kernel, tile_z, tile_x, shot_count,...  17.4 us
    all_to_all x1, waiting for transfers between devices, shards(): lax.all_to_all(cross, 'slab', split_axis=2, concat_axis=1, tiled=True)  16.2 us
    unnamed x31, local copies, waits for them, and re-layouts  8.25 us
    ppermute x2, waiting for transfers between devices, extended(): lax.ppermute(lax.slice_in_dim(block, 0, width, axis=dim), axis, backward)  7.5 us
    reduce_sum x1, other arithmetic, shards(): jnp.sum(source_field.astype(jnp.float32) * receiver_field.astype(jnp.floa...  6.85 us
    ppermute x2, starting transfers between devices, extended(): lax.ppermute(lax.slice_in_dim(block, block.shape[dim] - width, None, axis...  6.56 us
    all_to_all x1, starting transfers between devices, shards(): lax.all_to_all(cross, 'slab', split_axis=2, concat_axis=1, tiled=True)  6.35 us
    all_to_all x1, starting transfers between devices, shards(): tile = lax.all_to_all(rows, 'shot', split_axis=1, concat_axis=0, tiled=True)  5.54 us
  transfers between devices with their start and end apart: 6, of which 4 were waited for; matrix products, arithmetic and copies ran while one was open for 22% of the time, Pallas kernels for 0%

profile of v1, /device:TPU:1, one launch (start us, length us, event | category | flops | bytes accessed | tf_op | source)
XLA Modules:
  0.0 99.4 jit_solution(16733543481282405525)
XLA Ops:
  0.0 6.9 %multiply_reduce_fusion = bf16[3,4,256,128]{3,2,1,0:T(8,128)(2,1)S(1)} fusion(bf16[3,8,4,256,128]{4,3,2,1,0:T(8,128)(2,1)} %param.8, bf16[3,8,4,256,128]{4,3,2,1,0:T(8,128)(2,1)} %param.7), kind=kLoop, calls=%fused_computation.1 | loop fusion | flops 12189696 | bytes 13369344 | tf_op jit(solution)/shard_map/reduce_sum | solution.py:146
  6.9 1.5 %copy.51 = bf16[3,4,256,128]{3,1,0,2:T(4,128)(2,1)} copy(bf16[3,4,256,128]{3,2,1,0:T(8,128)(2,1)S(1)} %multiply_reduce_fusion) | data formatting | bytes 1572864 | tf_op jit(solution)/shard_map/convert_element_type | solution.py:148
  8.4 6.4 %all-to-all-start = ((bf16[3,4,256,128]{3,1,0,2:T(4,128)(2,1)}), bf16[3,4,256,128]{3,1,0,2:T(4,128)(2,1)S(1)}, u32[]{:S(2)}, u32[]{:S(2)}) async-start(bf16[3,4,256,128]{3,1,0,2:T(4,128)(2,1)} %copy.51), calls=%async_computation | async-start | bytes 1572864 | tf_op jit(solution)/shard_map/all_to_all | solution.py:149
  14.8 0.2 copy.62
  14.9 0.2 reshape.19
  15.1 0.6 gather_fusion
  15.8 0.1 bitcast_dynamic-update-slice_fusion.12
  15.9 0.1 bitcast_dynamic-update-slice_fusion.11
  16.0 0.1 bitcast_dynamic-update-slice_fusion.10
  16.0 0.1 bitcast_dynamic-update-slice_fusion.9
  16.3 1.2 %copy-done.2 = bf16[8,32,3,10,96]{4,1,3,2,0:T(8,128)(2,1)} copy-done((bf16[8,32,3,10,96]{4,1,3,2,0:T(8,128)(2,1)}, bf16[8,32,3,10,96]{4,1,3,2,0:T(8,128)(2,1)S(1)}, u32[]{:S(2)}) %copy-start.2) | copy-done | bytes 1474584
  17.5 0.1 select_bitcast_fusion
  17.6 16.2 %all-to-all-done = bf16[3,4,256,128]{3,1,0,2:T(4,128)(2,1)S(1)} async-done(((bf16[3,4,256,128]{3,1,0,2:T(4,128)(2,1)}), bf16[3,4,256,128]{3,1,0,2:T(4,128)(2,1)S(1)}, u32[]{:S(2)}, u32[]{:S(2)}) %all-to-all-start) | async-done | bytes 786464 | tf_op jit(solution)/shard_map/all_to_all | solution.py:149
  33.8 0.1 copy.52
  34.0 0.1 copy.53
  34.1 1.0 copy.54
  35.0 5.5 %all-to-all-start.1 = ((bf16[3,32,32,128]{3,2,0,1:T(8,128)(2,1)}), bf16[3,32,32,128]{3,2,0,1:T(8,128)(2,1)S(1)}, u32[]{:S(2)}, u32[]{:S(2)}) async-start(bf16[3,32,32,128]{3,2,0,1:T(8,128)(2,1)} %copy.54), calls=%async_computation.1 | async-start | bytes 1572864 | tf_op jit(solution)/shard_map/all_to_all | solution.py:150
  40.5 0.7 bitcast_dynamic-update-slice_fusion.6
  41.3 4.2 %copy.63 = bf16[32,8,3,10,96]{4,3,2,1,0:T(8,128)(2,1)} copy(bf16[32,8,3,10,96]{4,0,3,2,1:T(8,128)(2,1)} %bitcast.61) | data formatting | bytes 2949120 | tf_op jit(solution)/shard_map/transpose | solution.py:120
  45.5 3.9 %reshape.20.w2 = bf16[256,2880]{1,0:T(8,128)(2,1)S(1)} reshape(bf16[32,8,3,10,96]{4,3,2,1,0:T(8,128)(2,1)} %copy.63) | data formatting | bytes 2949120 | tf_op jit(solution)/shard_map/reshape | solution.py:120
  49.5 0.8 bitcast_dynamic-update-slice_fusion.5
  50.2 0.8 bitcast_dynamic-update-slice_fusion.4
  51.0 0.8 bitcast_dynamic-update-slice_fusion.3
  51.7 0.8 bitcast_dynamic-update-slice_fusion.2
  52.5 0.9 copy-done.1
  53.4 1.2 %copy.56 = bf16[4,3,8,32,128]{4,3,2,1,0:T(8,128)(2,1)S(1)} copy(bf16[4,3,8,32,128]{4,3,1,2,0:T(8,128)(2,1)} %bitcast.58) | data formatting | bytes 1572864 | tf_op jit(solution)/shard_map/all_to_all | solution.py:150
  54.7 0.1 copy.69
  54.8 3.5 %collective-permute-start = (bf16[12,2,32,128]{3,0,2,1:T(8,128)(2,1)S(1)}, bf16[12,2,32,128]{3,0,2,1:T(8,128)(2,1)}, u32[]{:S(2)}, u32[]{:S(2)}) collective-permute-start(bf16[12,2,32,128]{3,0,2,1:T(8,128)(2,1)S(1)} %copy.69), channel_id=1, source_target_pairs={{0,8},{8,16},{16,24},{1,9},{9,17},{17,25},{2,10},{10,18},{18,26},{... | collective-permute-start | bytes 589832 | tf_op jit(solution)/shard_map/ppermute | solution.py:19
  58.4 0.8 bitcast_dynamic-update-slice_fusion.1
  59.1 0.8 bitcast_dynamic-update-slice_fusion
  59.9 2.7 %copy.61 = bf16[6,32,3,8,48]{4,3,2,1,0:T(8,128)(2,1)} copy(bf16[6,32,3,8,48]{1,4,3,2,0:T(8,128)(2,1)} %bitcast_dynamic-update-slice_fusion) | data formatting | bytes 884736 | tf_op jit(solution)/shard_map/stack | solution.py:31
  62.6 2.1 %reshape.18.w1 = bf16[192,1152]{1,0:T(8,128)(2,1)S(1)} reshape(bf16[6,32,3,8,48]{4,3,2,1,0:T(8,128)(2,1)} %copy.61) | data formatting | bytes 884736 | tf_op jit(solution)/shard_map/reshape | solution.py:117
  64.7 0.1 broadcast_in_dim.22
  64.8 0.1 broadcast_in_dim_reshape.4.b2
  64.9 0.1 copy.64.b1
  65.0 0.1 copy.70
  65.1 1.9 %collective-permute-start.1 = (bf16[12,2,32,128]{3,0,2,1:T(8,128)(2,1)S(1)}, bf16[12,2,32,128]{3,0,2,1:T(8,128)(2,1)S(1)}, u32[]{:S(2)}, u32[]{:S(2)}) collective-permute-start(bf16[12,2,32,128]{3,0,2,1:T(8,128)(2,1)S(1)} %copy.70), channel_id=1, source_target_pairs={{8,0},{16,8},{24,16},{9,1},{17,9},{25,17},{10,2},{18,10},{26,18},{... | collective-permute-start | bytes 589832 | tf_op jit(solution)/shard_map/ppermute | solution.py:22
  67.1 1.0 constant_dynamic-update-slice_fusion.2
  68.0 0.6 constant_dynamic-update-slice_fusion.1
  68.7 4.2 %collective-permute-done.1 = bf16[12,2,32,128]{3,0,2,1:T(8,128)(2,1)S(1)} collective-permute-done((bf16[12,2,32,128]{3,0,2,1:T(8,128)(2,1)S(1)}, bf16[12,2,32,128]{3,0,2,1:T(8,128)(2,1)S(1)}, u32[]{:S(2)}, u32[]{:S(2)}) %collective-permute-start.1) | collective-permute-done | bytes 196640 | tf_op jit(solution)/shard_map/ppermute | solution.py:22
  72.9 3.0 %collective-permute-start.2 = (bf16[12,12,2,128]{3,0,2,1:T(8,128)(2,1)S(1)}, bf16[12,12,2,128]{3,0,2,1:T(8,128)(2,1)S(1)}, u32[]{:S(2)}, u32[]{:S(2)}) collective-permute-start(bf16[12,12,2,128]{3,0,2,1:T(8,128)(2,1)S(1)} %get-tuple-element.5), channel_id=1, source_target_pairs={{0,1},{1,2},{2,3},{3,4},{4,5},{5,6},{6,7},{8,9},{9,10},{10,11},{11... | collective-permute-start | bytes 221192 | tf_op jit(solution)/shard_map/ppermute | solution.py:19
  75.9 1.5 %collective-permute-start.3 = (bf16[12,12,2,128]{3,0,2,1:T(8,128)(2,1)S(1)}, bf16[12,12,2,128]{3,0,2,1:T(8,128)(2,1)S(1)}, u32[]{:S(2)}, u32[]{:S(2)}) collective-permute-start(bf16[12,12,2,128]{3,0,2,1:T(8,128)(2,1)S(1)} %get-tuple-element.6), channel_id=1, source_target_pairs={{1,0},{2,1},{3,2},{4,3},{5,4},{6,5},{7,6},{9,8},{10,9},{11,10},{12... | collective-permute-start | bytes 221192 | tf_op jit(solution)/shard_map/ppermute | solution.py:22
  77.4 0.1 pad_add_fusion.place
  77.5 0.5 collective-permute-done.2
  77.9 3.3 %collective-permute-done.3 = bf16[12,12,2,128]{3,0,2,1:T(8,128)(2,1)S(1)} collective-permute-done((bf16[12,12,2,128]{3,0,2,1:T(8,128)(2,1)S(1)}, bf16[12,12,2,128]{3,0,2,1:T(8,128)(2,1)S(1)}, u32[]{:S(2)}, u32[]{:S(2)}) %collective-permute-start.3) | collective-permute-done | bytes 73760 | tf_op jit(solution)/shard_map/ppermute | solution.py:22
  81.3 0.3 maximum_bitcast_fusion
  81.6 0.3 pad.64.img
  82.0 17.4 %convolutions.1 = bf16[32,8,32,128]{3,2,1,0:T(8,128)(2,1)} custom-call(s32[2]{0:T(128)S(1)} %pad_add_fusion.place, bf16[12,38,16,128]{3,2,1,0:T(8,128)(2,1)S(1)} %pad.64.img, bf16[192,1152]{1,0:T(8,128)(2,1)S(1)} %reshape.18.w1, f32[32,1]{1,0:T(8,128)S(1)} %copy.64.b1, bf16[256,2880]{1,0:T(8,128)(2,1)S(1)} %reshape.20.w2, ...), custom_call_target="tpu_custom_call" | custom-call | tf_op jit(solution)/shard_map/convolutions/pallas_call | solution.py:125
  (25 shorter events, 0.3 us)
Async XLA Ops:
  0.0 15.1 %copy-start = (bf16[32,12,3,3,3]{0,4,3,2,1:T(4,128)(2,1)S(1)}, bf16[32,12,3,3,3]{0,4,3,2,1:T(4,128)(2,1)}, u32[]{:S(2)}) copy-start(bf16[32,12,3,3,3]{0,4,3,2,1:T(4,128)(2,1)} %param.10) | copy-start | bytes 62212
  6.9 7.9 %copy-start.3 = (bf16[32,32,3,3,3]{1,0,4,3,2:T(8,128)(2,1)S(1)}, bf16[32,32,3,3,3]{1,0,4,3,2:T(8,128)(2,1)}, u32[]{:S(2)}) copy-start(bf16[32,32,3,3,3]{1,0,4,3,2:T(8,128)(2,1)} %param.12) | copy-start | bytes 165892
  6.9 8.2 %copy-start.6 = (s32[12]{0:T(128)S(1)}, s32[12]{0:T(128)}, u32[]{:S(2)}) copy-start(s32[12]{0:T(128)} %param.9) | copy-start | bytes 148
  8.4 25.4 %all-to-all-start = ((bf16[3,4,256,128]{3,1,0,2:T(4,128)(2,1)}), bf16[3,4,256,128]{3,1,0,2:T(4,128)(2,1)S(1)}, u32[]{:S(2)}, u32[]{:S(2)}) async-start(bf16[3,4,256,128]{3,1,0,2:T(4,128)(2,1)} %copy.51), calls=%async_computation | async-start | bytes 1572864 | tf_op jit(solution)/shard_map/all_to_all | solution.py:149
  16.2 1.3 %copy-start.2 = (bf16[8,32,3,10,96]{4,1,3,2,0:T(8,128)(2,1)}, bf16[8,32,3,10,96]{4,1,3,2,0:T(8,128)(2,1)S(1)}, u32[]{:S(2)}) copy-start(bf16[8,32,3,10,96]{4,1,3,2,0:T(8,128)(2,1)S(1)} %bitcast_dynamic-update-slice_fusion.7) | copy-start | bytes 4423684
  35.0 17.5 %all-to-all-start.1 = ((bf16[3,32,32,128]{3,2,0,1:T(8,128)(2,1)}), bf16[3,32,32,128]{3,2,0,1:T(8,128)(2,1)S(1)}, u32[]{:S(2)}, u32[]{:S(2)}) async-start(bf16[3,32,32,128]{3,2,0,1:T(8,128)(2,1)} %copy.54), calls=%async_computation.1 | async-start | bytes 1572864 | tf_op jit(solution)/shard_map/all_to_all | solution.py:150
  52.5 0.9 copy-start.1
  54.8 12.3 %collective-permute-start = (bf16[12,2,32,128]{3,0,2,1:T(8,128)(2,1)S(1)}, bf16[12,2,32,128]{3,0,2,1:T(8,128)(2,1)}, u32[]{:S(2)}, u32[]{:S(2)}) collective-permute-start(bf16[12,2,32,128]{3,0,2,1:T(8,128)(2,1)S(1)} %copy.69), channel_id=1, source_target_pairs={{0,8},{8,16},{16,24},{1,9},{9,17},{17,25},{2,10},{10,18},{18,26},{... | collective-permute-start | bytes 589832 | tf_op jit(solution)/shard_map/ppermute | solution.py:19
  59.9 4.9 %copy-start.4 = (f32[32]{0:T(128)S(1)}, f32[32]{0:T(128)}, u32[]{:S(2)}) copy-start(f32[32]{0:T(128)} %param.13) | copy-start | bytes 388
  59.9 5.0 %copy-start.5 = (f32[32]{0:T(128)S(1)}, f32[32]{0:T(128)}, u32[]{:S(2)}) copy-start(f32[32]{0:T(128)} %param.11) | copy-start | bytes 388
  65.1 7.7 %collective-permute-start.1 = (bf16[12,2,32,128]{3,0,2,1:T(8,128)(2,1)S(1)}, bf16[12,2,32,128]{3,0,2,1:T(8,128)(2,1)S(1)}, u32[]{:S(2)}, u32[]{:S(2)}) collective-permute-start(bf16[12,2,32,128]{3,0,2,1:T(8,128)(2,1)S(1)} %copy.70), channel_id=1, source_target_pairs={{8,0},{16,8},{24,16},{9,1},{17,9},{25,17},{10,2},{18,10},{26,18},{... | collective-permute-start | bytes 589832 | tf_op jit(solution)/shard_map/ppermute | solution.py:22
  72.9 5.0 %collective-permute-start.2 = (bf16[12,12,2,128]{3,0,2,1:T(8,128)(2,1)S(1)}, bf16[12,12,2,128]{3,0,2,1:T(8,128)(2,1)S(1)}, u32[]{:S(2)}, u32[]{:S(2)}) collective-permute-start(bf16[12,12,2,128]{3,0,2,1:T(8,128)(2,1)S(1)} %get-tuple-element.5), channel_id=1, source_target_pairs={{0,1},{1,2},{2,3},{3,4},{4,5},{5,6},{6,7},{8,9},{9,10},{10,11},{11... | collective-permute-start | bytes 221192 | tf_op jit(solution)/shard_map/ppermute | solution.py:19
  75.9 5.4 %collective-permute-start.3 = (bf16[12,12,2,128]{3,0,2,1:T(8,128)(2,1)S(1)}, bf16[12,12,2,128]{3,0,2,1:T(8,128)(2,1)S(1)}, u32[]{:S(2)}, u32[]{:S(2)}) collective-permute-start(bf16[12,12,2,128]{3,0,2,1:T(8,128)(2,1)S(1)} %get-tuple-element.6), channel_id=1, source_target_pairs={{1,0},{2,1},{3,2},{4,3},{5,4},{6,5},{7,6},{9,8},{10,9},{11,10},{12... | collective-permute-start | bytes 221192 | tf_op jit(solution)/shard_map/ppermute | solution.py:22

commit v2 on v1

--- a/solution.py
+++ b/solution.py
@@ -11,27 +11,171 @@
 OUT = 8
 
 
-def extended(block, sides, width):
-    for axis, dim in sides:
-        count = lax.axis_size(axis)
-        forward = [(i, i + 1) for i in range(count - 1)]
-        backward = [(target, source) for source, target in forward]
-        low = lax.ppermute(
-            lax.slice_in_dim(block, block.shape[dim] - width, None, axis=dim), axis, forward
+def exchange_kernel(shot_count, slab_count, slab_z, sent, got, send_sem, recv_sem, side_send, side_recv):
+    shot, slab = lax.axis_index("shot"), lax.axis_index("slab")
+    per_tile = slab_count // shot_count
+    tile_z = slab_z * per_tile
+    owner = slab // per_tile
+    mine = slab % per_tile
+
+    def place(shot_at, slab_at):
+        return {"shot": shot_at, "slab": slab_at}
+
+    def is_me(shot_at, slab_at):
+        return jnp.logical_and(shot_at == shot, slab_at == slab)
+
+    barrier = pltpu.get_barrier_semaphore()
+
+    def greet(shot_at, slab_at):
+        pl.semaphore_signal(
+            barrier, inc=1, device_id=place(shot_at, slab_at), device_id_type=pl.DeviceIdType.MESH
         )
-        high = lax.ppermute(lax.slice_in_dim(block, 0, width, axis=dim), axis, backward)
-        block = jnp.concatenate([low, block, high], axis=dim)
-    return block
-
-
-def banded(weight, count):
-    rows = [
-        jnp.pad(weight, ((0, 0), (0, 0), (i, count - 1 - i), (0, 0))) for i in range(count)
-    ]
-    return jnp.stack(rows), rows[0].shape[1] * rows[0].shape[2] * rows[0].shape[3]
-
-
-def conv_kernel(tile_z, tile_x, shot_count, slab_count, place, img, w1, b1, w2, b2, out, wide, hidden):
+
+    for source in range(shot_count):
+        for r in range(per_tile):
+            source_slab = shot * per_tile + r
+
+            @pl.when(jnp.logical_not(is_me(source, source_slab)))
+            def _():
+                greet(source, source_slab)
+
+    @pl.when(shot > 0)
+    def _():
+        greet(shot - 1, slab)
+
+    @pl.when(shot < shot_count - 1)
+    def _():
+        greet(shot + 1, slab)
+
+    partners = (
+        slab_count
+        - (owner == shot).astype(jnp.int32)
+        + (shot > 0).astype(jnp.int32)
+        + (shot < shot_count - 1).astype(jnp.int32)
+    )
+    pl.semaphore_wait(barrier, partners)
+
+    def slot(source, r):
+        return got.at[source, pl.ds(2 + r * slab_z, slab_z)]
+
+    def remote(k):
+        target = lax.rem(slab + slab_count // 2 + k, slab_count)
+        copy = pltpu.make_async_remote_copy(
+            src_ref=sent.at[target],
+            dst_ref=slot(shot, mine),
+            send_sem=send_sem.at[k],
+            recv_sem=recv_sem.at[shot, mine],
+            device_id=place(owner, target),
+            device_id_type=pl.DeviceIdType.MESH,
+        )
+        return target, copy
+
+    def local(target):
+        return pltpu.make_async_copy(
+            sent.at[target], slot(shot, mine), recv_sem.at[shot, mine]
+        )
+
+    for k in range(slab_count):
+        target, copy = remote(k)
+        self_copy = is_me(owner, target)
+
+        @pl.when(jnp.logical_not(self_copy))
+        def _():
+            copy.start()
+
+        @pl.when(self_copy)
+        def _():
+            local(target).start()
+
+    def arrived(r):
+        for source in range(shot_count):
+            pltpu.make_async_copy(slot(source, r), slot(source, r), recv_sem.at[source, r]).wait()
+
+    def side(low):
+        start, end = (2, tile_z + 2) if low else (tile_z, 0)
+        index = 0 if low else 1
+        return pltpu.make_async_remote_copy(
+            src_ref=got.at[:, pl.ds(start, 2)],
+            dst_ref=got.at[:, pl.ds(end, 2)],
+            send_sem=side_send.at[index],
+            recv_sem=side_recv.at[index],
+            device_id=place(shot - 1 if low else shot + 1, slab),
+            device_id_type=pl.DeviceIdType.MESH,
+        )
+
+    has_low, has_high = shot > 0, shot < shot_count - 1
+    arrived(0)
+
+    @pl.when(has_low)
+    def _():
+        side(True).start()
+
+    for r in range(1, per_tile):
+        arrived(r)
+
+    @pl.when(has_high)
+    def _():
+        side(False).start()
+
+    for k in range(slab_count):
+        target, copy = remote(k)
+
+        @pl.when(jnp.logical_not(is_me(owner, target)))
+        def _():
+            copy.wait_send()
+
+    @pl.when(has_low)
+    def _():
+        side(True).wait_send()
+        low = got.at[:, pl.ds(0, 2)]
+        pltpu.make_async_copy(low, low, side_recv.at[1]).wait()
+
+    @pl.when(has_high)
+    def _():
+        side(False).wait_send()
+        high = got.at[:, pl.ds(tile_z + 2, 2)]
+        pltpu.make_async_copy(high, high, side_recv.at[0]).wait()
+
+
+def exchange(sent, slab_z):
+    shot_count, slab_count = lax.axis_size("shot"), lax.axis_size("slab")
+    per_tile = slab_count // shot_count
+    tile_z = slab_z * per_tile
+    anywhere = pl.BlockSpec(memory_space=pl.ANY)
+    return pl.pallas_call(
+        functools.partial(exchange_kernel, shot_count, slab_count, slab_z),
+        out_shape=jax.ShapeDtypeStruct(
+            (shot_count, tile_z + 4) + sent.shape[2:], jnp.bfloat16
+        ),
+        in_specs=[anywhere],
+        out_specs=anywhere,
+        scratch_shapes=[
+            pltpu.SemaphoreType.DMA((slab_count,)),
+            pltpu.SemaphoreType.DMA((shot_count, per_tile)),
+            pltpu.SemaphoreType.DMA((2,)),
+            pltpu.SemaphoreType.DMA((2,)),
+        ],
+        compiler_params=pltpu.CompilerParams(collective_id=0, has_side_effects=True),
+        name="exchange",
+    )(sent)
+
+
+def spread(weight, count, lanes):
+    base = jnp.pad(weight, ((0, 0), (0, 0), (0, count - 1), (0, 0)))
+    base = base.reshape(base.shape[0], -1).astype(jnp.float32)
+    return jnp.pad(base, ((0, 0), (0, lanes - base.shape[1])))
+
+
+def lanes_for(size):
+    return -(-size // 128) * 128
+
+
+def banded(base, count, step):
+    rows = [base] + [pltpu.roll(base, i * step, 1) for i in range(1, count)]
+    return jnp.concatenate([r.astype(jnp.bfloat16) for r in rows], axis=0)
+
+
+def conv_kernel(tile_z, tile_x, shot_count, slab_count, place, img, base1, b1, base2, b2, out, wide, hidden, w1, w2):
     half = tile_z // 2
     y = img.shape[3]
     lanes = 2 * y
@@ -40,7 +184,18 @@
     cell = lane - upper * y
     first = cell == 0
     last = cell == y - 1
-    channels = w1.shape[0] // WIDE
+    channels = base1.shape[0]
+    out_channels = out.shape[0]
+    w1[...] = banded(base1[...], WIDE, 3 * img.shape[2])[:, : w1.shape[1]]
+    rows = banded(base2[...], OUT, 3 * channels)
+    count = rows.shape[0]
+    to = lax.broadcasted_iota(jnp.int32, (count, count), 0)
+    source = lax.broadcasted_iota(jnp.int32, (count, count), 1)
+    moved = (to % OUT) * out_channels + to // OUT == source
+    swap = jnp.where(moved, 1.0, 0.0).astype(jnp.bfloat16)
+    w2[...] = jnp.dot(swap, rows, preferred_element_type=jnp.float32).astype(jnp.bfloat16)[
+        :, : w2.shape[1]
+    ]
 
     def three(values):
         left = jnp.where(first, 0.0, pltpu.roll(values, 1, 1))
@@ -81,7 +236,6 @@
                 for k, part in enumerate(three(value)):
                     hidden[z, x, k * channels:(k + 1) * channels, :] = part
 
-    out_channels = out.shape[0]
     chunk = min(16, tile_x)
 
     @pl.loop(0, half)
@@ -113,11 +267,11 @@
     hidden_x = -(-(tile_x + 2) // WIDE) * WIDE
     w1 = jnp.transpose(first_weight, (0, 2, 3, 4, 1))
     w1 = jnp.pad(w1, ((0, 0),) * 4 + ((0, depth - inputs),)).reshape(channels, 3, 3, 3 * depth)
-    w1, k1 = banded(w1, WIDE)
-    w1 = w1.reshape(WIDE * channels, k1)
+    k1 = 3 * (WIDE + 2) * 3 * depth
+    w1 = spread(w1, WIDE, lanes_for(k1))
     w2 = jnp.transpose(second_weight, (0, 2, 3, 4, 1)).reshape(out_channels, 3, 3, 3 * channels)
-    w2, k2 = banded(w2, OUT)
-    w2 = jnp.transpose(w2, (1, 0, 2, 3, 4)).reshape(out_channels * OUT, k2)
+    k2 = 3 * (OUT + 2) * 3 * channels
+    w2 = spread(w2, OUT, lanes_for(k2))
     b1 = first_bias[:, None]
     b2 = jnp.repeat(second_bias, OUT)[:, None]
     place = jnp.stack([lax.axis_index("shot"), lax.axis_index("slab")]).astype(jnp.int32)
@@ -130,6 +284,8 @@
         scratch_shapes=[
             pltpu.VMEM((half + 4, image.shape[1], 3 * depth, 2 * y), jnp.bfloat16),
             pltpu.VMEM((half + 2, hidden_x, 3 * channels, 2 * y), jnp.bfloat16),
+            pltpu.VMEM((WIDE * channels, k1), jnp.bfloat16),
+            pltpu.VMEM((OUT * out_channels, k2), jnp.bfloat16),
         ],
         compiler_params=pltpu.CompilerParams(vmem_limit_bytes=48 * 1024 * 1024),
         name="convolutions",
@@ -146,15 +302,26 @@
     cross = jnp.sum(
         source_field.astype(jnp.float32) * receiver_field.astype(jnp.float32), axis=1
     ).astype(jnp.bfloat16)
-    rows = lax.all_to_all(cross, "slab", split_axis=2, concat_axis=1, tiled=True)
-    tile = lax.all_to_all(rows, "shot", split_axis=1, concat_axis=0, tiled=True)
-    padded = extended(tile, (("shot", 1), ("slab", 2)), 2)
+    wide_x = tile_x + 4
+    cross = jnp.pad(cross, ((0, 0), (0, 0), (2, 2), (0, 0)))
+    tiles = jnp.stack(
+        [cross[:, :, t * tile_x:t * tile_x + wide_x] for t in range(slab_count)]
+    )
+    packed = shots_here * wide_x
+    spare = -(-packed // 16) * 16 - packed
+    sent = jnp.transpose(tiles, (0, 2, 1, 3, 4)).reshape(slab_count, slab_z, packed, -1)
+    sent = jnp.pad(sent, ((0, 0), (0, 0), (0, spare), (0, 0)))
+    got = exchange(sent, slab_z)[:, :, :packed]
+    z_place = lax.axis_index("shot") * tile_z - 2 + jnp.arange(tile_z + 4, dtype=jnp.int32)
+    z_valid = (z_place >= 0) & (z_place < tile_z * shot_count)
+    got = jnp.where(z_valid[None, :, None, None], got, jnp.zeros_like(got))
+    got = got.reshape(shot_count, tile_z + 4, shots_here, wide_x, -1)
+    shots = shot_count * shots_here
+    image = jnp.transpose(got, (1, 3, 0, 2, 4)).reshape(tile_z + 4, wide_x, shots, -1)
     hidden_x = -(-(tile_x + 2) // WIDE) * WIDE
-    image = jnp.transpose(padded, (1, 2, 0, 3))
-    shots = image.shape[2]
     depth = -(-shots // 16) * 16
     image = jnp.pad(
-        image, ((0, 0), (0, hidden_x + 2 - image.shape[1]), (0, depth - shots), (0, 0))
+        image, ((0, 0), (0, hidden_x + 2 - wide_x), (0, depth - shots), (0, 0))
     )
     weight_of_shot = jnp.take(first_weight, shot_group, axis=1)
     return convolutions(

time: 99.9 us -> 66.8 us (0.67)
  the two profiles are of different devices: /device:TPU:1 before, /device:TPU:11 now
where the time goes in v2:
time: 66.8 us; the launch traced here: 66.6 us
  Pallas kernels  49.5 us (74%)
  other arithmetic  9.93 us (15%)
  local copies, waits for them, and re-layouts  7.06 us (11%)
    pallas_call x1, Pallas kernels, exchange(): pl.pallas_call(functools.partial(exchange_kernel, shot_count, slab_count,...  31.4 us
    pallas_call x1, Pallas kernels, convolutions(): pl.pallas_call(functools.partial(conv_kernel, tile_z, tile_x, shot_count,...  18.1 us
    reduce_sum x1, other arithmetic, shards(): jnp.sum(source_field.astype(jnp.float32) * receiver_field.astype(jnp.floa...  6.83 us
    select_n x1, other arithmetic, shards(): got = jnp.where(z_valid[None, :, None, None], got, jnp.zeros_like(got))  1.5 us

profile of v2, /device:TPU:11, one launch (start us, length us, event | category | flops | bytes accessed | tf_op | source)
XLA Modules:
  0.0 66.6 jit_solution(14278851569642160052)
XLA Ops:
  0.0 0.0 copy-start
  0.0 0.1 pad_add_fusion.place
  0.1 0.7 compare_and_fusion
  0.7 0.7 compare_select_fusion
  1.4 0.7 %copy.62.b1 = f32[32,1]{1,0:T(8,128)S(1)} copy(f32[32,1]{0,1:T(1,128)} %bitcast.53) | data formatting | bytes 256 | tf_op jit(solution)/shard_map/broadcast_in_dim | solution.py:275
  2.1 0.7 %broadcast_in_dim.36 = f32[32,8]{1,0:T(8,128)S(1)} broadcast(f32[32]{0:T(128)} %param.13), dimensions={0} | broadcast | bytes 1152 | tf_op jit(solution)/shard_map/broadcast_in_dim | solution.py:276
  2.9 0.0 copy-done
  2.9 0.0 copy-start.1
  2.9 0.6 gather_fusion
  3.5 0.1 select_bitcast_fusion
  3.7 0.1 copy.59
  3.9 0.1 broadcast_in_dim_reshape.4.b2
  4.0 0.2 reshape.38.base1
  4.2 0.0 copy-done.1
  4.2 0.2 copy.67
  4.3 0.2 reshape.48
  4.5 0.1 pad.35.clone
  4.6 0.3 convert_element_type.37
  4.9 6.8 %multiply_reduce_fusion = bf16[3,4,256,128]{3,2,1,0:T(8,128)(2,1)S(1)} fusion(bf16[3,8,4,256,128]{4,3,2,1,0:T(8,128)(2,1)} %param.8, bf16[3,8,4,256,128]{4,3,2,1,0:T(8,128)(2,1)} %param.7), kind=kLoop, calls=%fused_computation.1 | loop fusion | flops 12189696 | bytes 13369344 | tf_op jit(solution)/shard_map/reduce_sum | solution.py:302
  11.8 0.1 fusion.9
  11.9 0.1 fusion.8
  11.9 0.1 fusion.7
  12.0 0.1 fusion.6
  12.0 0.1 fusion.5
  12.1 0.1 fusion.4
  12.1 0.1 fusion.3
  12.2 0.3 copy.53
  12.5 0.1 copy.54
  12.7 1.0 %pad.31.sent = bf16[8,4,112,128]{3,2,1,0:T(8,128)(2,1)} pad(bf16[8,4,108,128]{3,2,1,0:T(8,128)(2,1)S(1)} %copy.54, bf16[]{:T(256)} %constant.36.clone.1), padding=0_0x0_0x0_4x0_0 | pad | bytes 1802242 | tf_op jit(solution)/shard_map/jit(_pad)/pad | solution.py:313
  13.7 31.4 %exchange.1 = bf16[4,12,112,128]{3,2,1,0:T(8,128)(2,1)} custom-call(bf16[8,4,112,128]{3,2,1,0:T(8,128)(2,1)} %pad.31.sent), custom_call_target="tpu_custom_call" | custom-call | tf_op jit(solution)/shard_map/exchange/pallas_call | solution.py:145
  45.1 1.5 %slice_select_fusion = bf16[4,12,108,128]{3,2,1,0:T(8,128)(2,1)S(1)} fusion(bf16[4,12,112,128]{3,2,1,0:T(8,128)(2,1)} %exchange.1, pred[12]{0:T(512)(128)(4,1)S(1)} %compare_and_fusion.1), kind=kLoop, calls=%fused_computation.2 | loop fusion | flops 663552 | bytes 2654220 | tf_op jit(solution)/shard_map/jit(_where)/select_n | solution.py:317
  46.6 1.0 %copy.55 = bf16[4,12,108,128]{3,0,2,1:T(4,128)(2,1)S(1)} copy(bf16[4,12,108,128]{3,2,1,0:T(8,128)(2,1)S(1)} %slice_select_fusion) | data formatting | bytes 2654208 | tf_op jit(solution)/shard_map/jit(_where)/select_n | solution.py:317
  47.6 0.2 copy.56
  47.8 0.4 copy.57
  48.2 0.3 pad.32.img
  48.6 18.1 %convolutions.1 = bf16[32,8,32,128]{3,2,1,0:T(8,128)(2,1)} custom-call(s32[2]{0:T(128)S(1)} %pad_add_fusion.place, bf16[12,38,16,128]{3,2,1,0:T(8,128)(2,1)S(1)} %pad.32.img, f32[32,1152]{1,0:T(8,128)S(1)} %reshape.38.base1, f32[32,1]{1,0:T(8,128)S(1)} %copy.62.b1, f32[32,2944]{1,0:T(8,128)S(1)} %pad_convert_fusion.1.base2, ...), custom_call_target="tpu_custom_call" | custom-call | tf_op jit(solution)/shard_map/convolutions/pallas_call | solution.py:279
  (7 shorter events, 0.2 us)
Async XLA Ops:
  0.0 2.9 %copy-start = (bf16[32,12,3,3,3]{0,4,3,2,1:T(4,128)(2,1)S(1)}, bf16[32,12,3,3,3]{0,4,3,2,1:T(4,128)(2,1)}, u32[]{:S(2)}) copy-start(bf16[32,12,3,3,3]{0,4,3,2,1:T(4,128)(2,1)} %param.10) | copy-start | bytes 62212
  2.9 1.3 %copy-start.1 = (bf16[32,32,3,3,3]{1,0,4,3,2:T(8,128)(2,1)S(1)}, bf16[32,32,3,3,3]{1,0,4,3,2:T(8,128)(2,1)}, u32[]{:S(2)}) copy-start(bf16[32,32,3,3,3]{1,0,4,3,2:T(8,128)(2,1)} %param.12) | copy-start | bytes 165892

commit v3 on v2

--- a/solution.py
+++ b/solution.py
@@ -11,7 +11,15 @@
 OUT = 8
 
 
-def exchange_kernel(shot_count, slab_count, slab_z, sent, got, send_sem, recv_sem, side_send, side_recv):
+def exchange_kernel(
+    shot_count, slab_count, tile_x, source, receiver, got,
+    source_part, receiver_part, edged, sent, load_sem, send_sem, recv_sem, side_send, side_recv,
+):
+    shots_here, steps, slab_z, all_x, _ = source.shape
+    chunk_x = source_part.shape[4]
+    per_chunk = chunk_x // tile_x
+    chunks = all_x // chunk_x
+    wide_x = tile_x + 4
     shot, slab = lax.axis_index("shot"), lax.axis_index("slab")
     per_tile = slab_count // shot_count
     tile_z = slab_z * per_tile
@@ -24,6 +32,24 @@
     def is_me(shot_at, slab_at):
         return jnp.logical_and(shot_at == shot, slab_at == slab)
 
+    def chunk_at(k):
+        return lax.rem(slab // per_chunk + chunks // 2 - 1 + k, chunks)
+
+    def loads(k):
+        rows = pl.ds(pl.multiple_of(chunk_at(k) * chunk_x, chunk_x), chunk_x)
+        return [
+            pltpu.make_async_copy(
+                field.at[:, :, :, rows], part.at[k], load_sem.at[i, k]
+            )
+            for i, (field, part) in enumerate(
+                ((source, source_part), (receiver, receiver_part))
+            )
+        ]
+
+    for k in range(chunks):
+        for copy in loads(k):
+            copy.start()
+
     barrier = pltpu.get_barrier_semaphore()
 
     def greet(shot_at, slab_at):
@@ -31,13 +57,13 @@
             barrier, inc=1, device_id=place(shot_at, slab_at), device_id_type=pl.DeviceIdType.MESH
         )
 
-    for source in range(shot_count):
+    for from_shot in range(shot_count):
         for r in range(per_tile):
-            source_slab = shot * per_tile + r
-
-            @pl.when(jnp.logical_not(is_me(source, source_slab)))
+            from_slab = shot * per_tile + r
+
+            @pl.when(jnp.logical_not(is_me(from_shot, from_slab)))
             def _():
-                greet(source, source_slab)
+                greet(from_shot, from_slab)
 
     @pl.when(shot > 0)
     def _():
@@ -55,41 +81,76 @@
     )
     pl.semaphore_wait(barrier, partners)
 
-    def slot(source, r):
-        return got.at[source, pl.ds(2 + r * slab_z, slab_z)]
-
-    def remote(k):
-        target = lax.rem(slab + slab_count // 2 + k, slab_count)
+    def slot(from_shot, r):
+        return got.at[from_shot, pl.ds(2 + r * slab_z, slab_z)]
+
+    def remote(n):
+        target = chunk_at(n // per_chunk) * per_chunk + n % per_chunk
         copy = pltpu.make_async_remote_copy(
-            src_ref=sent.at[target],
+            src_ref=sent.at[n],
             dst_ref=slot(shot, mine),
-            send_sem=send_sem.at[k],
+            send_sem=send_sem.at[n],
             recv_sem=recv_sem.at[shot, mine],
             device_id=place(owner, target),
             device_id_type=pl.DeviceIdType.MESH,
         )
         return target, copy
 
-    def local(target):
-        return pltpu.make_async_copy(
-            sent.at[target], slot(shot, mine), recv_sem.at[shot, mine]
-        )
-
-    for k in range(slab_count):
-        target, copy = remote(k)
-        self_copy = is_me(owner, target)
-
-        @pl.when(jnp.logical_not(self_copy))
-        def _():
-            copy.start()
-
-        @pl.when(self_copy)
-        def _():
-            local(target).start()
+    def multiply(k):
+        for copy in loads(k):
+            copy.wait()
+        first = chunk_at(k) * per_chunk + 1
+
+        @pl.loop(0, slab_z)
+        def _(z):
+            for l in range(shots_here):
+                total = None
+                for t in range(steps):
+                    term = source_part[k, l, t, z].astype(jnp.float32) * receiver_part[
+                        k, l, t, z
+                    ].astype(jnp.float32)
+                    total = term if total is None else total + term
+                row = l * wide_x
+                for j in range(per_chunk):
+                    part = total[j * tile_x:(j + 1) * tile_x]
+                    edged[first + j, z, row + 2:row + 2 + tile_x] = part
+                    edged[first + j + 1, z, row:row + 2] = part[tile_x - 2:]
+                    edged[first + j - 1, z, row + 2 + tile_x:row + wide_x] = part[:2]
+
+    def send(k):
+        for j in range(per_chunk):
+            n = k * per_chunk + j
+            target, copy = remote(n)
+
+            @pl.loop(0, slab_z)
+            def _(z):
+                sent[n, z] = edged[target + 1, z].astype(sent.dtype)
+
+            self_copy = is_me(owner, target)
+
+            @pl.when(jnp.logical_not(self_copy))
+            def _():
+                copy.start()
+
+            @pl.when(self_copy)
+            def _():
+                pltpu.make_async_copy(
+                    sent.at[n], slot(shot, mine), recv_sem.at[shot, mine]
+                ).start()
+
+    for z in range(slab_z):
+        edged[:, z] = jnp.zeros_like(edged[:, z])
+    for k in range(chunks):
+        multiply(k)
+        if k >= 2:
+            send(k - 1)
+    send(chunks - 1)
+    send(0)
 
     def arrived(r):
-        for source in range(shot_count):
-            pltpu.make_async_copy(slot(source, r), slot(source, r), recv_sem.at[source, r]).wait()
+        for from_shot in range(shot_count):
+            here = slot(from_shot, r)
+            pltpu.make_async_copy(here, here, recv_sem.at[from_shot, r]).wait()
 
     def side(low):
         start, end = (2, tile_z + 2) if low else (tile_z, 0)
@@ -117,8 +178,8 @@
     def _():
         side(False).start()
 
-    for k in range(slab_count):
-        target, copy = remote(k)
+    for n in range(slab_count):
+        target, copy = remote(n)
 
         @pl.when(jnp.logical_not(is_me(owner, target)))
         def _():
@@ -137,27 +198,38 @@
         pltpu.make_async_copy(high, high, side_recv.at[0]).wait()
 
 
-def exchange(sent, slab_z):
+def exchange(source, receiver):
+    shots_here, steps, slab_z, all_x, y = source.shape
     shot_count, slab_count = lax.axis_size("shot"), lax.axis_size("slab")
     per_tile = slab_count // shot_count
     tile_z = slab_z * per_tile
+    tile_x = all_x // slab_count
+    chunk_x = max(tile_x, 16)
+    chunks = all_x // chunk_x
+    packed = -(-shots_here * (tile_x + 4) // 16) * 16
     anywhere = pl.BlockSpec(memory_space=pl.ANY)
+    part = pltpu.VMEM((chunks, shots_here, steps, slab_z, chunk_x, y), jnp.bfloat16)
     return pl.pallas_call(
-        functools.partial(exchange_kernel, shot_count, slab_count, slab_z),
-        out_shape=jax.ShapeDtypeStruct(
-            (shot_count, tile_z + 4) + sent.shape[2:], jnp.bfloat16
-        ),
-        in_specs=[anywhere],
+        functools.partial(exchange_kernel, shot_count, slab_count, tile_x),
+        out_shape=jax.ShapeDtypeStruct((shot_count, tile_z + 4, packed, y), jnp.bfloat16),
+        in_specs=[anywhere] * 2,
         out_specs=anywhere,
         scratch_shapes=[
+            part,
+            part,
+            pltpu.VMEM((slab_count + 2, slab_z, packed, y), jnp.float32),
+            pltpu.VMEM((slab_count, slab_z, packed, y), jnp.bfloat16),
+            pltpu.SemaphoreType.DMA((2, chunks)),
             pltpu.SemaphoreType.DMA((slab_count,)),
             pltpu.SemaphoreType.DMA((shot_count, per_tile)),
             pltpu.SemaphoreType.DMA((2,)),
             pltpu.SemaphoreType.DMA((2,)),
         ],
-        compiler_params=pltpu.CompilerParams(collective_id=0, has_side_effects=True),
+        compiler_params=pltpu.CompilerParams(
+            collective_id=0, has_side_effects=True, vmem_limit_bytes=56 * 1024 * 1024
+        ),
         name="exchange",
-    )(sent)
+    )(source, receiver)
 
 
 def spread(weight, count, lanes):
@@ -170,12 +242,19 @@
     return -(-size // 128) * 128
 
 
+def column(row, repeats):
+    count = row.shape[1]
+    to = lax.broadcasted_iota(jnp.int32, (count * repeats, count), 0) // repeats
+    source = lax.broadcasted_iota(jnp.int32, (count * repeats, count), 1)
+    return jnp.sum(jnp.where(to == source, row, 0.0), axis=1, keepdims=True)
+
+
 def banded(base, count, step):
     rows = [base] + [pltpu.roll(base, i * step, 1) for i in range(1, count)]
     return jnp.concatenate([r.astype(jnp.bfloat16) for r in rows], axis=0)
 
 
-def conv_kernel(tile_z, tile_x, shot_count, slab_count, place, img, base1, b1, base2, b2, out, wide, hidden, w1, w2):
+def conv_kernel(tile_z, tile_x, shot_count, slab_count, place, img, base1, bias1, base2, bias2, out, wide, hidden, w1, w2):
     half = tile_z // 2
     y = img.shape[3]
     lanes = 2 * y
@@ -187,6 +266,8 @@
     channels = base1.shape[0]
     out_channels = out.shape[0]
     w1[...] = banded(base1[...], WIDE, 3 * img.shape[2])[:, : w1.shape[1]]
+    b1 = column(bias1[...], 1)
+    b2 = column(bias2[...], OUT)
     rows = banded(base2[...], OUT, 3 * channels)
     count = rows.shape[0]
     to = lax.broadcasted_iota(jnp.int32, (count, count), 0)
@@ -231,7 +312,7 @@
                 x_place = x_base + x
                 x_valid = jnp.logical_and(x_place >= 0, x_place < tile_x * slab_count)
                 valid = jnp.logical_and(z_valid, x_valid)
-                value = jnp.maximum(got[i * channels:(i + 1) * channels] + b1[...], 0.0)
+                value = jnp.maximum(got[i * channels:(i + 1) * channels] + b1, 0.0)
                 value = jnp.where(valid, value, 0.0)
                 for k, part in enumerate(three(value)):
                     hidden[z, x, k * channels:(k + 1) * channels, :] = part
@@ -248,7 +329,7 @@
                 got = jnp.dot(
                     w2[...], window.reshape(-1, lanes), preferred_element_type=jnp.float32
                 )
-                parts.append(jnp.maximum(got + b2[...], 0.0))
+                parts.append(jnp.maximum(got + b2, 0.0))
             for h in range(2):
                 pieces = [
                     p[:, h * y:(h + 1) * y].reshape(out_channels, OUT, y) for p in parts
@@ -272,8 +353,8 @@
     w2 = jnp.transpose(second_weight, (0, 2, 3, 4, 1)).reshape(out_channels, 3, 3, 3 * channels)
     k2 = 3 * (OUT + 2) * 3 * channels
     w2 = spread(w2, OUT, lanes_for(k2))
-    b1 = first_bias[:, None]
-    b2 = jnp.repeat(second_bias, OUT)[:, None]
+    b1 = first_bias[None]
+    b2 = second_bias[None]
     place = jnp.stack([lax.axis_index("shot"), lax.axis_index("slab")]).astype(jnp.int32)
     vmem = pl.BlockSpec(memory_space=pltpu.VMEM)
     return pl.pallas_call(
@@ -299,19 +380,9 @@
     shot_count, slab_count = lax.axis_size("shot"), lax.axis_size("slab")
     tile_z = slab_z * slab_count // shot_count
     tile_x = all_x // slab_count
-    cross = jnp.sum(
-        source_field.astype(jnp.float32) * receiver_field.astype(jnp.float32), axis=1
-    ).astype(jnp.bfloat16)
     wide_x = tile_x + 4
-    cross = jnp.pad(cross, ((0, 0), (0, 0), (2, 2), (0, 0)))
-    tiles = jnp.stack(
-        [cross[:, :, t * tile_x:t * tile_x + wide_x] for t in range(slab_count)]
-    )
     packed = shots_here * wide_x
-    spare = -(-packed // 16) * 16 - packed
-    sent = jnp.transpose(tiles, (0, 2, 1, 3, 4)).reshape(slab_count, slab_z, packed, -1)
-    sent = jnp.pad(sent, ((0, 0), (0, 0), (0, spare), (0, 0)))
-    got = exchange(sent, slab_z)[:, :, :packed]
+    got = exchange(source_field, receiver_field)[:, :, :packed]
     z_place = lax.axis_index("shot") * tile_z - 2 + jnp.arange(tile_z + 4, dtype=jnp.int32)
     z_valid = (z_place >= 0) & (z_place < tile_z * shot_count)
     got = jnp.where(z_valid[None, :, None, None], got, jnp.zeros_like(got))
@@ -323,7 +394,7 @@
     image = jnp.pad(
         image, ((0, 0), (0, hidden_x + 2 - wide_x), (0, depth - shots), (0, 0))
     )
-    weight_of_shot = jnp.take(first_weight, shot_group, axis=1)
+    weight_of_shot = first_weight.at[:, shot_group].get(mode="promise_in_bounds")
     return convolutions(
         image, weight_of_shot, first_bias, second_weight, second_bias, tile_z, tile_x
     )

time: 66.8 us -> 57.2 us (0.86)
  other arithmetic: 9.93 us -> 2.32 us
  local copies, waits for them, and re-layouts: 7.06 us -> 4.57 us
    reduce_sum x1 -> x0, other arithmetic: 6.83 us -> none  [shards(): jnp.sum(source_field.astype(jnp.float32) * receiver_field.astype(jnp.floa...]
    broadcast_in_dim x2 -> x0, local copies, waits for them, and re-layouts: 1.46 us -> none  [the longest x1 0.74 us: convolutions(): b1 = first_bias[:, None]]
    pad x1 -> x0, local copies, waits for them, and re-layouts: 1.01 us -> none  [shards(): sent = jnp.pad(sent, ((0, 0), (0, 0), (0, spare), (0, 0)))]
    unnamed x14 -> x11, local copies, waits for them, and re-layouts: 0.74 us -> 1.34 us
where the time goes in v3:
time: 57.2 us; the launch traced here: 57 us
  Pallas kernels  50 us (87%)
  local copies, waits for them, and re-layouts  4.57 us (8%)
  other arithmetic  2.32 us (4%)
    pallas_call x1, Pallas kernels, exchange(): pl.pallas_call(functools.partial(exchange_kernel, shot_count, slab_count,...  32 us
    pallas_call x1, Pallas kernels, convolutions(): pl.pallas_call(functools.partial(conv_kernel, tile_z, tile_x, shot_count,...  18 us
    select_n x1, other arithmetic, shards(): got = jnp.where(z_valid[None, :, None, None], got, jnp.zeros_like(got))  1.5 us
    unnamed x11, local copies, waits for them, and re-layouts  1.34 us

profile of v3, /device:TPU:11, one launch (start us, length us, event | category | flops | bytes accessed | tf_op | source)
XLA Modules:
  0.0 57.0 jit_solution(10073228165322654979)
XLA Ops:
  0.0 0.0 copy-start
  0.0 0.1 pad_add_fusion.place
  0.1 0.7 %compare_select_fusion = s32[12]{0:T(128)S(1)} fusion(s32[12]{0:T(128)} %param.9), kind=kLoop, calls=%fused_computation.5 | loop fusion | flops 36 | bytes 96 | tf_op jit(solution)/shard_map/select_n | solution.py:397
  0.8 0.1 copy-done
  0.9 0.6 %gather_fusion = bf16[12,32,3,3,3]{1,4,3,2,0:T(4,128)(2,1)S(1)} fusion(bf16[32,12,3,3,3]{0,4,3,2,1:T(4,128)(2,1)S(1)} %copy-done, s32[1024]{0:T(1024)S(1)} %pad_clamp_fusion), kind=kCustom, calls=%fused_computation | custom fusion | bytes 41520 | tf_op jit(solution)/shard_map/gather | solution.py:397
  1.5 0.0 copy-start.3
  1.6 0.1 copy.20
  1.8 0.2 reshape.29.base1
  2.0 0.5 copy-done.3
  2.5 0.2 copy.25
  2.6 0.2 reshape.39
  2.8 0.1 pad.25.clone
  2.9 0.3 convert_element_type.21
  3.2 32.0 %exchange.1 = bf16[4,12,112,128]{3,2,1,0:T(8,128)(2,1)} custom-call(bf16[3,8,4,256,128]{4,3,2,1,0:T(8,128)(2,1)} %source.1, bf16[3,8,4,256,128]{4,3,2,1,0:T(8,128)(2,1)} %receiver.1), custom_call_target="tpu_custom_call" | custom-call | tf_op jit(solution)/shard_map/exchange/pallas_call | solution.py:212
  35.2 1.5 %slice_select_fusion = bf16[4,12,108,128]{3,2,1,0:T(8,128)(2,1)S(1)} fusion(bf16[4,12,112,128]{3,2,1,0:T(8,128)(2,1)} %exchange.1, pred[12]{0:T(512)(128)(4,1)S(1)} %compare_and_fusion), kind=kLoop, calls=%fused_computation.1 | loop fusion | flops 663552 | bytes 2654220 | tf_op jit(solution)/shard_map/jit(_where)/select_n | solution.py:388
  36.7 1.0 %copy.16 = bf16[4,12,108,128]{3,0,2,1:T(4,128)(2,1)S(1)} copy(bf16[4,12,108,128]{3,2,1,0:T(8,128)(2,1)S(1)} %slice_select_fusion) | data formatting | bytes 2654208 | tf_op jit(solution)/shard_map/jit(_where)/select_n | solution.py:388
  37.7 0.2 copy.17
  38.0 0.4 copy.18
  38.3 0.0 copy-start.1
  38.3 0.0 copy-start.2
  38.4 0.3 pad.22.img
  38.7 0.3 copy-done.1
  39.0 0.0 copy-done.2
  39.0 18.0 %convolutions.1 = bf16[32,8,32,128]{3,2,1,0:T(8,128)(2,1)} custom-call(s32[2]{0:T(128)S(1)} %pad_add_fusion.place, bf16[12,38,16,128]{3,2,1,0:T(8,128)(2,1)S(1)} %pad.22.img, f32[32,1152]{1,0:T(8,128)S(1)} %reshape.29.base1, f32[1,32]{1,0:T(1,128)S(1)} %bitcast.13, f32[32,2944]{1,0:T(8,128)S(1)} %pad_convert_fusion.1.base2, f32[1,32]{1,0:T(1,128)S(1)} %bitcast.14), custom_call_target="tpu_custom_call" | custom-call | tf_op jit(solution)/shard_map/convolutions/pallas_call | solution.py:360
  (6 shorter events, 0.1 us)
Async XLA Ops:
  0.0 0.9 %copy-start = (bf16[32,12,3,3,3]{0,4,3,2,1:T(4,128)(2,1)S(1)}, bf16[32,12,3,3,3]{0,4,3,2,1:T(4,128)(2,1)}, u32[]{:S(2)}) copy-start(bf16[32,12,3,3,3]{0,4,3,2,1:T(4,128)(2,1)} %param.10) | copy-start | bytes 62212
  1.5 0.9 %copy-start.3 = (bf16[32,32,3,3,3]{1,0,4,3,2:T(8,128)(2,1)S(1)}, bf16[32,32,3,3,3]{1,0,4,3,2:T(8,128)(2,1)}, u32[]{:S(2)}) copy-start(bf16[32,32,3,3,3]{1,0,4,3,2:T(8,128)(2,1)} %param.12) | copy-start | bytes 165892
  38.3 0.7 %copy-start.1 = (f32[32]{0:T(128)S(1)}, f32[32]{0:T(128)}, u32[]{:S(2)}) copy-start(f32[32]{0:T(128)} %param.11) | copy-start | bytes 388
  38.3 0.7 %copy-start.2 = (f32[32]{0:T(128)S(1)}, f32[32]{0:T(128)}, u32[]{:S(2)}) copy-start(f32[32]{0:T(128)} %param.13) | copy-start | bytes 388

commit v4 on v3

--- a/solution.py
+++ b/solution.py
@@ -254,9 +254,12 @@
     return jnp.concatenate([r.astype(jnp.bfloat16) for r in rows], axis=0)
 
 
-def conv_kernel(tile_z, tile_x, shot_count, slab_count, place, img, base1, bias1, base2, bias2, out, wide, hidden, w1, w2):
+def conv_kernel(
+    tile_z, tile_x, shot_count, slab_count, shots_here,
+    place, got, base1, bias1, base2, bias2, out, wide, hidden, w1, w2, plane,
+):
     half = tile_z // 2
-    y = img.shape[3]
+    y = got.shape[3]
     lanes = 2 * y
     lane = lax.broadcasted_iota(jnp.int32, (1, lanes), 1)
     upper = (lane >= y).astype(jnp.int32)
@@ -265,7 +268,7 @@
     last = cell == y - 1
     channels = base1.shape[0]
     out_channels = out.shape[0]
-    w1[...] = banded(base1[...], WIDE, 3 * img.shape[2])[:, : w1.shape[1]]
+    w1[...] = banded(base1[...], WIDE, 1)[:, : w1.shape[1]]
     b1 = column(bias1[...], 1)
     b2 = column(bias2[...], OUT)
     rows = banded(base2[...], OUT, 3 * channels)
@@ -283,27 +286,40 @@
         right = jnp.where(last, 0.0, pltpu.roll(values, lanes - 1, 1))
         return [v.astype(jnp.bfloat16) for v in (left, values, right)]
 
-    depth = img.shape[2]
+    wide_x = tile_x + 4
+    depth = wide.shape[2] // 3
+    hidden_x = hidden.shape[1]
 
     @pl.loop(0, half + 4)
     def _(z):
-        for x in range(img.shape[1]):
-            pair = jnp.concatenate(
-                [img[z, x].astype(jnp.float32), img[z + half, x].astype(jnp.float32)], axis=1
-            )
-            for k, part in enumerate(three(pair)):
-                wide[z, x, k * depth:(k + 1) * depth, :] = part
+        for h in range(2):
+            z_at = place[0] * tile_z - 2 + z + h * half
+            here = jnp.logical_and(z_at >= 0, z_at < tile_z * shot_count)
+            for s in range(shot_count):
+                rows = got[s, z + h * half].astype(jnp.float32)
+                plane[h, s] = jnp.where(here, rows, 0.0)
+        for g in range(hidden_x // WIDE):
+            pieces = []
+            for s in range(shot_count):
+                for l in range(shots_here):
+                    row = l * wide_x + g * WIDE
+                    pieces.append(
+                        jnp.concatenate(
+                            [plane[h, s, row:row + WIDE + 2] for h in range(2)], axis=1
+                        )
+                    )
+            for k, part in enumerate(three(jnp.concatenate(pieces, axis=0))):
+                wide[z, g, k * depth:(k + 1) * depth, :] = part
 
     z_base = place[0] * tile_z - 1
     x_base = place[1] * tile_x - 1
-    hidden_x = hidden.shape[1]
 
     @pl.loop(0, half + 2)
     def _(z):
         z_place = z_base + z + upper * half
         z_valid = jnp.logical_and(z_place >= 0, z_place < tile_z * shot_count)
         for g in range(hidden_x // WIDE):
-            window = wide[pl.ds(z, 3), g * WIDE:g * WIDE + WIDE + 2]
+            window = wide[pl.ds(z, 3), g]
             got = jnp.dot(
                 w1[...], window.reshape(-1, lanes), preferred_element_type=jnp.float32
             )
@@ -338,18 +354,20 @@
                 out[:, z + h * half, c * chunk:(c + 1) * chunk, :] = block.astype(out.dtype)
 
 
-def convolutions(image, first_weight, first_bias, second_weight, second_bias, tile_z, tile_x):
+def convolutions(
+    got, first_weight, first_bias, second_weight, second_bias, tile_z, tile_x, shots_here
+):
     shot_count, slab_count = lax.axis_size("shot"), lax.axis_size("slab")
     channels, inputs = first_weight.shape[:2]
     out_channels = second_weight.shape[0]
-    y = image.shape[3]
-    depth = image.shape[2]
+    y = got.shape[3]
     half = tile_z // 2
     hidden_x = -(-(tile_x + 2) // WIDE) * WIDE
-    w1 = jnp.transpose(first_weight, (0, 2, 3, 4, 1))
-    w1 = jnp.pad(w1, ((0, 0),) * 4 + ((0, depth - inputs),)).reshape(channels, 3, 3, 3 * depth)
-    k1 = 3 * (WIDE + 2) * 3 * depth
-    w1 = spread(w1, WIDE, lanes_for(k1))
+    depth = inputs * (WIDE + 2)
+    k1 = 9 * depth
+    w1 = jnp.transpose(first_weight, (0, 2, 4, 1, 3))
+    w1 = jnp.pad(w1, ((0, 0),) * 4 + ((0, WIDE - 1),)).reshape(channels, k1)
+    w1 = jnp.pad(w1, ((0, 0), (0, lanes_for(k1) - k1))).astype(jnp.float32)
     w2 = jnp.transpose(second_weight, (0, 2, 3, 4, 1)).reshape(out_channels, 3, 3, 3 * channels)
     k2 = 3 * (OUT + 2) * 3 * channels
     w2 = spread(w2, OUT, lanes_for(k2))
@@ -358,19 +376,20 @@
     place = jnp.stack([lax.axis_index("shot"), lax.axis_index("slab")]).astype(jnp.int32)
     vmem = pl.BlockSpec(memory_space=pltpu.VMEM)
     return pl.pallas_call(
-        functools.partial(conv_kernel, tile_z, tile_x, shot_count, slab_count),
+        functools.partial(conv_kernel, tile_z, tile_x, shot_count, slab_count, shots_here),
         out_shape=jax.ShapeDtypeStruct((out_channels, tile_z, tile_x, y), jnp.bfloat16),
         in_specs=[pl.BlockSpec(memory_space=pltpu.SMEM)] + [vmem] * 5,
         out_specs=vmem,
         scratch_shapes=[
-            pltpu.VMEM((half + 4, image.shape[1], 3 * depth, 2 * y), jnp.bfloat16),
+            pltpu.VMEM((half + 4, hidden_x // WIDE, 3 * depth, 2 * y), jnp.bfloat16),
             pltpu.VMEM((half + 2, hidden_x, 3 * channels, 2 * y), jnp.bfloat16),
             pltpu.VMEM((WIDE * channels, k1), jnp.bfloat16),
             pltpu.VMEM((OUT * out_channels, k2), jnp.bfloat16),
+            pltpu.VMEM((2, shot_count) + got.shape[2:], jnp.float32),
         ],
         compiler_params=pltpu.CompilerParams(vmem_limit_bytes=48 * 1024 * 1024),
         name="convolutions",
-    )(place, image, w1, b1, w2, b2)
+    )(place, got, w1, b1, w2, b2)
 
 
 def shards(
@@ -380,23 +399,12 @@
     shot_count, slab_count = lax.axis_size("shot"), lax.axis_size("slab")
     tile_z = slab_z * slab_count // shot_count
     tile_x = all_x // slab_count
-    wide_x = tile_x + 4
-    packed = shots_here * wide_x
-    got = exchange(source_field, receiver_field)[:, :, :packed]
-    z_place = lax.axis_index("shot") * tile_z - 2 + jnp.arange(tile_z + 4, dtype=jnp.int32)
-    z_valid = (z_place >= 0) & (z_place < tile_z * shot_count)
-    got = jnp.where(z_valid[None, :, None, None], got, jnp.zeros_like(got))
-    got = got.reshape(shot_count, tile_z + 4, shots_here, wide_x, -1)
-    shots = shot_count * shots_here
-    image = jnp.transpose(got, (1, 3, 0, 2, 4)).reshape(tile_z + 4, wide_x, shots, -1)
-    hidden_x = -(-(tile_x + 2) // WIDE) * WIDE
-    depth = -(-shots // 16) * 16
-    image = jnp.pad(
-        image, ((0, 0), (0, hidden_x + 2 - wide_x), (0, depth - shots), (0, 0))
+    got = exchange(source_field, receiver_field)
+    weight_of_shot = first_weight.at[:, shot_group].get(
+        mode="promise_in_bounds", wrap_negative_indices=False
     )
-    weight_of_shot = first_weight.at[:, shot_group].get(mode="promise_in_bounds")
     return convolutions(
-        image, weight_of_shot, first_bias, second_weight, second_bias, tile_z, tile_x
+        got, weight_of_shot, first_bias, second_weight, second_bias, tile_z, tile_x, shots_here
     )
 
 

time: 57.2 us -> 54.4 us (0.951)
  local copies, waits for them, and re-layouts: 4.57 us -> 2.99 us
  other arithmetic: 2.32 us -> 0.85 us
    select_n x2 -> x0, other arithmetic: 2.15 us -> none  [the longest x1 1.5 us: shards(): got = jnp.where(z_valid[None, :, None, None], got, jnp.zeros_like(got))]
    select_n x1 -> x0, local copies, waits for them, and re-layouts: 1.03 us -> none  [shards(): got = jnp.where(z_valid[None, :, None, None], got, jnp.zeros_like(got))]
    gather x1, other arithmetic: 0.01 us -> 0.74 us  [shards(): first_weight.at[:, shot_group]]
    unnamed x11 -> x13, local copies, waits for them, and re-layouts: 1.34 us -> 1.82 us
where the time goes in v4:
time: 54.4 us; the launch traced here: 54.2 us
  Pallas kernels  50.3 us (92%)
  local copies, waits for them, and re-layouts  2.99 us (5%)
  other arithmetic  0.85 us (2%)
    pallas_call x1, Pallas kernels, exchange(): pl.pallas_call(functools.partial(exchange_kernel, shot_count, slab_count,...  32 us
    pallas_call x1, Pallas kernels, convolutions(): pl.pallas_call(functools.partial(conv_kernel, tile_z, tile_x, shot_count,...  18.3 us
    unnamed x13, local copies, waits for them, and re-layouts  1.82 us

profile of v4, /device:TPU:11, one launch (start us, length us, event | category | flops | bytes accessed | tf_op | source)
XLA Modules:
  0.0 54.2 jit_solution(16136761239519149674)
XLA Ops:
  0.0 0.0 copy-start
  0.0 0.0 copy-start.4
  0.0 0.1 pad_add_fusion.place
  0.1 0.7 %pad_clamp_fusion = s32[1024]{0:T(1024)S(1)} fusion(s32[12]{0:T(128)} %param.9), kind=kLoop, calls=%fused_computation.3 | loop fusion | flops 1024 | bytes 4144 | tf_op jit(solution)/shard_map/gather | solution.py:403
  0.8 0.1 copy-done
  0.9 0.6 %gather_fusion = bf16[12,32,3,3,3]{1,4,3,2,0:T(4,128)(2,1)S(1)} fusion(bf16[32,12,3,3,3]{0,4,3,2,1:T(4,128)(2,1)S(1)} %copy-done, s32[1024]{0:T(1024)S(1)} %pad_clamp_fusion), kind=kCustom, calls=%fused_computation | custom fusion | bytes 41520 | tf_op jit(solution)/shard_map/gather | solution.py:403
  1.6 0.1 pad.18.clone
  1.7 0.1 copy.10
  1.8 0.0 copy-done.4
  1.8 0.2 copy.15
  2.0 0.2 reshape.20
  2.2 0.1 pad.20.clone
  2.3 0.3 convert_element_type.16
  2.6 0.0 copy-start.2
  2.6 0.0 copy-start.3
  2.6 32.0 %exchange.1.got = bf16[4,12,112,128]{3,2,1,0:T(8,128)(2,1)} custom-call(bf16[3,8,4,256,128]{4,3,2,1,0:T(8,128)(2,1)} %source.1, bf16[3,8,4,256,128]{4,3,2,1,0:T(8,128)(2,1)} %receiver.1), custom_call_target="tpu_custom_call" | custom-call | tf_op jit(solution)/shard_map/exchange/pallas_call | solution.py:212
  34.6 0.0 copy-done.2
  34.6 0.0 copy-done.3
  34.6 0.0 copy-start.1
  34.6 1.3 %copy-done.1 = bf16[4,12,112,128]{3,2,1,0:T(8,128)(2,1)S(1)} copy-done((bf16[4,12,112,128]{3,2,1,0:T(8,128)(2,1)S(1)}, bf16[4,12,112,128]{3,2,1,0:T(8,128)(2,1)}, u32[]{:S(2)}) %copy-start.1) | copy-done | bytes 1376280
  35.9 18.3 %convolutions.1 = bf16[32,8,32,128]{3,2,1,0:T(8,128)(2,1)} custom-call(s32[2]{0:T(128)S(1)} %pad_add_fusion.place, bf16[4,12,112,128]{3,2,1,0:T(8,128)(2,1)S(1)} %copy-done.1, f32[32,896]{1,0:T(8,128)S(1)} %pad_convert_fusion.1.base1, f32[1,32]{1,0:T(1,128)S(1)} %bitcast.7, f32[32,2944]{1,0:T(8,128)S(1)} %pad_convert_fusion.base2, f32[1,32]{1,0:T(1,128)S(1)} %bitcast.8), custom_call_target="tpu_custom_call" | custom-call | tf_op jit(solution)/shard_map/convolutions/pallas_call | solution.py:378
  (3 shorter events, 0.1 us)
Async XLA Ops:
  0.0 0.9 %copy-start = (bf16[32,12,3,3,3]{0,4,3,2,1:T(4,128)(2,1)S(1)}, bf16[32,12,3,3,3]{0,4,3,2,1:T(4,128)(2,1)}, u32[]{:S(2)}) copy-start(bf16[32,12,3,3,3]{0,4,3,2,1:T(4,128)(2,1)} %param.10) | copy-start | bytes 62212
  0.0 1.8 %copy-start.4 = (bf16[32,32,3,3,3]{1,0,4,3,2:T(8,128)(2,1)S(1)}, bf16[32,32,3,3,3]{1,0,4,3,2:T(8,128)(2,1)}, u32[]{:S(2)}) copy-start(bf16[32,32,3,3,3]{1,0,4,3,2:T(8,128)(2,1)} %param.12) | copy-start | bytes 165892
  2.6 32.0 %copy-start.2 = (f32[32]{0:T(128)S(1)}, f32[32]{0:T(128)}, u32[]{:S(2)}) copy-start(f32[32]{0:T(128)} %param.11) | copy-start | bytes 388
  2.6 32.0 %copy-start.3 = (f32[32]{0:T(128)S(1)}, f32[32]{0:T(128)}, u32[]{:S(2)}) copy-start(f32[32]{0:T(128)} %param.13) | copy-start | bytes 388
  34.6 1.3 %copy-start.1 = (bf16[4,12,112,128]{3,2,1,0:T(8,128)(2,1)S(1)}, bf16[4,12,112,128]{3,2,1,0:T(8,128)(2,1)}, u32[]{:S(2)}) copy-start(bf16[4,12,112,128]{3,2,1,0:T(8,128)(2,1)} %exchange.1.got) | copy-start | bytes 4128772
